TPU v7x, 32 devices: a whole 2x2x4 slice. The times are simulated.
32 devices in a mesh: grp: 2 (over x), gs: 16 (over z, y, core).
Axes of the slice: x: 2, y: 2, z: 4, core: 2. Of those that a mesh axis runs over, the one named last changes fastest.
Arguments:
- centres: float32 [3, 131072], P(None, ('grp', 'gs')), parts along dimension 1, may hold values from -6 to 7, as said below
- factor: float32 [9, 131072], P(None, ('grp', 'gs')), parts along dimension 1, may hold values from -0.048 to 0.048
- harmonics: float32 [48, 131072], P(None, ('grp', 'gs')), parts along dimension 1, may hold values from -3.6 to 3.6
- opacity: float32 [131072], P(('grp', 'gs')), parts along dimension 0, may hold values from -4 to 0
- cameras: float32 [8, 3], P('grp'), parts along dimension 0, may hold values from -0.5 to 0.5, as said below
- requests: int32 [16384], P(('grp', 'gs')), parts along dimension 0, may hold values from -1 to 4095, as said below
- tile_lists: int32 [256, 512], P(('grp', 'gs')), parts along dimension 0, may hold values from -1 to 511, as said below
- tile_ids: int32 [256], P(('grp', 'gs')), parts along dimension 0, may hold values from 0 to 7919, as said below
- image_cotangent: float32 [3, 256, 256], P(None, ('grp', 'gs')), parts along dimension 1, may hold values from -6 to 6
Outputs:
- image: float32 [3, 256, 256], P(None, ('grp', 'gs')), parts along dimension 1
- grad_centres: float32 [3, 131072], P(None, ('grp', 'gs')), parts along dimension 1
- grad_factor: float32 [9, 131072], P(None, ('grp', 'gs')), parts along dimension 1
- grad_harmonics: float32 [48, 131072], P(None, ('grp', 'gs')), parts along dimension 1
- grad_opacity: float32 [131072], P(('grp', 'gs')), parts along dimension 0
There are 2 independent parts, one for each index of `grp`. A program takes and returns all parts, laid end to end along the dimension named above; each array names one. Nothing has to cross between parts.
Inputs may be any that keep to these rules, and one draw needn't show every extreme that they name: `requests`: entry 512 * d + 32 * s + k names the k-th Gaussian (an index among owner s's 4096) that device d asks of owner s, or is -1; the named entries of each pair (d, s) come first. `tile_lists`: row t belongs to device t // 8; an entry r >= 0 names slot r mod 32 of owner r // 32 of that device's requests, and that request is not -1. Entries are in compositing order, front first; after the listed entries a row holds -1 to its end. `tile_ids`: distinct numbers; number v * 60 * 33 + 60 * y + x is tile column x, tile row y of view v. `cameras`: third coordinates lie within 0.25 of zero. `centres`: every centre's third coordinate exceeds every camera's third coordinate by 2.5 or more.
All inputs are finite; a program needn't handle non-finite values.
Results may differ from a plain program's by a relative error of at most 0.0003.
Values sent between devices are 32-bit elements; how exact they have to be, the bound alone decides.
A program may use at most 64 MiB of HBM per device.

v0:
```python
import functools

import jax
import jax.numpy as jnp
from jax import lax
from jax.experimental import pallas as pl
from jax.experimental.pallas import tpu as pltpu
from jax.sharding import PartitionSpec as P

TILE = 16
PIX = TILE * TILE
IMG_W = 960
IMG_H = 540
FOCAL = 600
TILES_ACROSS = 60
TILE_ROWS = 33
VIEWS = 4
CAP = 32
LANES = 128
SEGS = LANES // CAP
ROWS = 16
CHUNK = 512
F32 = jnp.float32
BF16 = jnp.bfloat16
VMEM_LIMIT = 48 * 1024 * 1024

BAND_ONE = 0.4886025119029199


def sh_basis(dir_x, dir_y, dir_z):
    sq_x = dir_x * dir_x
    sq_y = dir_y * dir_y
    sq_z = dir_z * dir_z
    return [
        jnp.full_like(dir_x, 0.28209479177387814),
        -BAND_ONE * dir_y,
        BAND_ONE * dir_z,
        -BAND_ONE * dir_x,
        1.0925484305920792 * dir_x * dir_y,
        -1.0925484305920792 * dir_y * dir_z,
        0.31539156525252005 * (2.0 * sq_z - sq_x - sq_y),
        -1.0925484305920792 * dir_x * dir_z,
        0.5462742152960396 * (sq_x - sq_y),
        -0.5900435899266435 * dir_y * (3.0 * sq_x - sq_y),
        2.890611442640554 * dir_x * dir_y * dir_z,
        -0.4570457994644658 * dir_y * (4.0 * sq_z - sq_x - sq_y),
        0.3731763325901154 * dir_z * (2.0 * sq_z - 3.0 * sq_x - 3.0 * sq_y),
        -0.4570457994644658 * dir_x * (4.0 * sq_z - sq_x - sq_y),
        1.445305721320277 * dir_z * (sq_x - sq_y),
        -0.5900435899266435 * dir_x * (sq_x - 3.0 * sq_y),
    ]


def geometry(pos, shape, cam):
    cov = [
        [
            shape[3 * i] * shape[3 * j]
            + shape[3 * i + 1] * shape[3 * j + 1]
            + shape[3 * i + 2] * shape[3 * j + 2]
            for j in range(3)
        ]
        for i in range(3)
    ]
    rel_x = pos[0] - cam[0]
    rel_y = pos[1] - cam[1]
    rel_z = pos[2] - cam[2]
    inverse = 1.0 / rel_z
    screen_x = FOCAL * rel_x * inverse + 0.5 * IMG_W
    screen_y = FOCAL * rel_y * inverse + 0.5 * IMG_H
    jac_xx = FOCAL * inverse
    jac_xz = -FOCAL * rel_x * inverse * inverse
    jac_yz = -FOCAL * rel_y * inverse * inverse
    cov_a = (
        jac_xx * jac_xx * cov[0][0]
        + 2.0 * jac_xx * jac_xz * cov[0][2]
        + jac_xz * jac_xz * cov[2][2]
        + 0.3
    )
    cov_b = (
        jac_xx * jac_xx * cov[0][1]
        + jac_xx * jac_yz * cov[0][2]
        + jac_xz * jac_xx * cov[2][1]
        + jac_xz * jac_yz * cov[2][2]
    )
    cov_c = (
        jac_xx * jac_xx * cov[1][1]
        + 2.0 * jac_xx * jac_yz * cov[1][2]
        + jac_yz * jac_yz * cov[2][2]
        + 0.3
    )
    scale = 1.0 / (cov_a * cov_c - cov_b * cov_b)
    shrink = 1.0 / jnp.sqrt(rel_x * rel_x + rel_y * rel_y + rel_z * rel_z)
    basis = sh_basis(rel_x * shrink, rel_y * shrink, rel_z * shrink)
    return [screen_x, screen_y, cov_c * scale, -cov_b * scale, cov_a * scale], basis


def split(value, parts):
    out = []
    for _ in range(parts - 1):
        piece = value.astype(BF16)
        out.append(piece)
        value = value - piece.astype(F32)
    out.append(value.astype(BF16))
    return out


def mm(a, b):
    return jnp.dot(a, b, preferred_element_type=F32)


def mm_nt(a, b):
    return lax.dot_general(a, b, (((1,), (1,)), ((), ())), preferred_element_type=F32)


def mm_tn(a, b):
    return lax.dot_general(a, b, (((0,), (0,)), ((), ())), preferred_element_type=F32)


def swap_segments(arrays):
    seg = lax.broadcasted_iota(jnp.int32, arrays[0].shape, 1) // CAP
    turned = [[a if s == 0 else pltpu.roll(a, CAP * s, 1) for s in range(SEGS)] for a in arrays]
    out = []
    for o in range(SEGS):
        z = turned[0][(0 - o) % SEGS]
        for v in range(1, SEGS):
            z = jnp.where(seg == v, turned[v][(v - o) % SEGS], z)
        out.append(z)
    return out


def one_hot(base, index, rows):
    ids = lax.broadcasted_iota(jnp.int32, (rows, index.shape[1]), 0) + base
    return jnp.where(ids == index, 1.0, 0.0).astype(BF16)


def raw_rows(raw):
    def row(i):
        return raw[i : i + 1]
    return (
        [row(57 + i) for i in range(3)],
        [row(48 + i) for i in range(9)],
        [row(i) for i in range(48)],
        row(60),
    )


def camera_columns(cam_ref):
    return [cam_ref[:, i : i + 1] for i in range(3)]


def project_kernel(want_ref, cen_ref, fac_ref, har_ref, opa_ref, cam_ref, rec_ref, raw_ref, parts_ref):
    gauss = cen_ref.shape[1]
    for base in range(0, gauss, CHUNK):
        cols = slice(base, base + CHUNK)
        whole = jnp.concatenate(
            [har_ref[:, cols], fac_ref[:, cols], cen_ref[:, cols], opa_ref[:, cols],
             jnp.zeros((3, CHUNK), F32)], axis=0)
        parts_ref[:, cols] = jnp.concatenate(split(whole, 3), axis=0)
    want = jnp.maximum(want_ref[...], 0)
    acc = jnp.zeros((192, CHUNK), F32)
    for base in range(0, gauss, CHUNK):
        acc = acc + mm(parts_ref[:, base : base + CHUNK], one_hot(base, want, CHUNK))
    raw = acc[0:64] + acc[64:128] + acc[128:192]
    raw_ref[...] = raw
    pos, shape, coeffs, logit = raw_rows(raw)
    records, basis = geometry(pos, shape, camera_columns(cam_ref))
    for c in range(3):
        summed = jnp.full_like(basis[0], 0.5)
        for j in range(16):
            summed = summed + basis[j] * coeffs[16 * c + j]
        records.append(summed)
    strength = 1.0 / (1.0 + jnp.exp(-logit))
    records.append(jnp.broadcast_to(strength, (VIEWS, CHUNK)))
    blank = jnp.zeros((ROWS - 9, CHUNK), F32)
    by_view = [jnp.concatenate([r[v : v + 1] for r in records] + [blank], axis=0) for v in range(VIEWS)]
    for b in range(CHUNK // LANES):
        swapped = swap_segments([x[:, b * LANES : (b + 1) * LANES] for x in by_view])
        for o in range(SEGS):
            rec_ref[b * SEGS + o] = swapped[o]


def pull_kernel(want_ref, back_ref, raw_ref, cam_ref, cen_ref, fac_ref, har_ref, opa_ref):
    gauss = cen_ref.shape[1]
    by_view = [[] for _ in range(VIEWS)]
    for b in range(CHUNK // LANES):
        swapped = swap_segments([back_ref[b * SEGS + o] for o in range(SEGS)])
        for v in range(VIEWS):
            by_view[v].append(swapped[v])
    by_view = [jnp.concatenate(x, axis=1) for x in by_view]
    grads = [jnp.concatenate([by_view[v][c : c + 1] for v in range(VIEWS)], axis=0) for c in range(9)]
    pos, shape, coeffs, logit = raw_rows(raw_ref[...])
    cam = camera_columns(cam_ref)
    (_, basis), pull = jax.vjp(lambda p, s: geometry(p, s, cam), pos, shape)
    basis_grads = []
    for j in range(16):
        total = grads[5] * coeffs[j]
        for c in range(1, 3):
            total = total + grads[5 + c] * coeffs[16 * c + j]
        basis_grads.append(total)
    pos_grads, shape_grads = pull((grads[:5], basis_grads))
    rows = [
        jnp.sum(grads[5 + c] * basis[j], axis=0, keepdims=True) for c in range(3) for j in range(16)
    ]
    rows += list(shape_grads) + list(pos_grads)
    keep = 1.0 - 1.0 / (1.0 + jnp.exp(-logit))
    rows.append(keep * jnp.sum(grads[8], axis=0, keepdims=True))
    rows.append(jnp.zeros((3, CHUNK), F32))
    parts = jnp.concatenate(split(jnp.concatenate(rows, axis=0), 2), axis=0)
    want = want_ref[...]
    first = pl.program_id(0) == 0
    for base in range(0, gauss, CHUNK):
        cols = slice(base, base + CHUNK)
        both = mm_nt(parts, one_hot(base, want, CHUNK))
        total = both[0:64] + both[64:128]

        def put(ref, value):
            @pl.when(first)
            def _():
                ref[:, cols] = value

            @pl.when(jnp.logical_not(first))
            def _():
                ref[:, cols] = ref[:, cols] + value

        put(har_ref, total[0:48])
        put(fac_ref, total[48:57])
        put(cen_ref, total[57:60])
        put(opa_ref, total[60:61])


def loop(count, body):
    if count == 1:
        body(0)
    else:
        def step(i, carry):
            body(i)
            return carry
        lax.fori_loop(0, count, step, 0)


def aligned(i, size):
    return i * size if isinstance(i, int) else pl.multiple_of(i * size, size)


def raster_kernel(
    ids_ref, rec_ref, list_ref, cot_ref, img_ref, back_ref,
    rec_s, sel_s, grad_s, lk_s, alpha_s, ratio_s, shade_s, before_s, w_s, sw_s, swp_s,
):
    owners = rec_ref.shape[0]
    slots = owners * CAP
    tiles, length = list_ref.shape
    half = length // 2

    def unpack(b):
        swapped = swap_segments([rec_ref[b * SEGS + o] for o in range(SEGS)])
        for v in range(VIEWS):
            rec_s[v, :, pl.ds(aligned(b, LANES), LANES)] = jnp.concatenate(split(swapped[v], 3), axis=0)

    if owners <= 16:
        for b in range(owners // SEGS):
            unpack(b)
    else:
        loop(owners // SEGS, unpack)
    grad_s[...] = jnp.zeros_like(grad_s)

    row_i = lax.broadcasted_iota(jnp.int32, (length, length), 0)
    col_i = lax.broadcasted_iota(jnp.int32, (length, length), 1)
    upper = jnp.where(row_i < col_i, 1.0, 0.0).astype(BF16)
    lower = jnp.where(row_i > col_i, 1.0, 0.0).astype(BF16)
    px = lax.broadcasted_iota(jnp.int32, (TILE, length), 0).astype(F32) + 0.5

    def tile(t):
        code = ids_ref[t]
        view = code // (TILES_ACROSS * TILE_ROWS)
        place = code - view * (TILES_ACROSS * TILE_ROWS)
        line = place // TILES_ACROSS
        corner_y = (line * TILE).astype(F32)
        corner_x = ((place - line * TILES_ACROSS) * TILE).astype(F32)
        entries = list_ref[pl.ds(t, 1), :]
        got = [jnp.zeros((3 * ROWS, length), F32)]

        def gather(c):
            at = pl.ds(aligned(c, CHUNK), CHUNK)
            sel = one_hot(c * CHUNK, entries, CHUNK)
            sel_s[at, :] = sel
            return mm(rec_s[view, :, at], sel)

        if slots == CHUNK:
            got = gather(0)
        else:
            got = lax.fori_loop(
                0, slots // CHUNK, lambda c, a: a + gather(c), jnp.zeros((3 * ROWS, length), F32))
        rec = got[0:ROWS] + got[ROWS : 2 * ROWS] + got[2 * ROWS :]
        con_a, con_b, con_c = rec[2:3], rec[3:4], rec[4:5]
        colour = rec[5:8]
        strength = rec[8:9]
        dx = (corner_x + px) - rec[0:1]
        dy = (corner_y + px) - rec[1:2]
        quad_x = (-0.5 * con_a) * dx * dx
        cross = (-con_b) * dx
        quad_y = (-0.5 * con_c) * dy * dy
        for y in range(TILE):
            rows = slice(y * TILE, (y + 1) * TILE)
            falloff = jnp.exp(quad_x + cross * dy[y : y + 1] + quad_y[y : y + 1])
            alpha = strength * falloff
            keep = jnp.log(1.0 - alpha)
            alpha_s[rows] = alpha
            ratio_s[rows] = alpha * jnp.exp(-keep)
            hi, lo = split(keep, 2)
            lk_s[0, rows] = hi
            lk_s[1, rows] = lo
        before_s[:, :half] = mm(lk_s[0, :, :half], upper[:half, :half]) + mm(
            lk_s[1, :, :half], upper[:half, :half])
        before_s[:, half:] = mm(lk_s[0], upper[:, half:]) + mm(lk_s[1], upper[:, half:])

        cot = jnp.concatenate([cot_ref[c, pl.ds(t, 1), :] for c in range(3)], axis=0)
        cot_hi, cot_lo = split(cot, 2)
        col_hi, col_lo = split(colour, 2)
        pad = jnp.zeros((ROWS - 9, PIX), BF16)
        shade_s[...] = mm_tn(
            jnp.concatenate([cot_hi, cot_hi, cot_lo, pad], axis=0),
            jnp.concatenate([col_hi, col_lo, col_hi, jnp.zeros((ROWS - 9, length), BF16)], axis=0),
        )
        for y in range(TILE):
            rows = slice(y * TILE, (y + 1) * TILE)
            weight = alpha_s[rows] * jnp.exp(before_s[rows])
            hi, lo = split(weight, 2)
            w_s[0, rows] = hi
            w_s[1, rows] = lo
            shaded = shade_s[rows] * weight
            sw_s[rows] = shaded
            hi, lo = split(shaded, 2)
            swp_s[0, rows] = hi
            swp_s[1, rows] = lo
        before_s[:, half:] = mm(swp_s[0, :, half:], lower[half:, half:]) + mm(
            swp_s[1, :, half:], lower[half:, half:])
        before_s[:, :half] = mm(swp_s[0], lower[:, :half]) + mm(swp_s[1], lower[:, :half])

        six = jnp.zeros((2, length), BF16)
        col_parts = jnp.concatenate([col_hi, col_lo, six], axis=0)
        by_hi = mm_nt(col_parts, w_s[0])
        by_lo = mm_nt(col_parts, w_s[1])
        image = by_hi[0:3] + by_hi[3:6] + by_lo[0:3]
        for c in range(3):
            img_ref[c, pl.ds(t, 1), :] = image[c : c + 1]
        cot_parts = jnp.concatenate([cot_hi, cot_lo, jnp.zeros((2, PIX), BF16)], axis=0)
        by_hi = mm(cot_parts, w_s[0])
        by_lo = mm(cot_parts, w_s[1])
        grad_colour = by_hi[0:3] + by_hi[3:6] + by_lo[0:3]

        sum_0 = jnp.zeros((TILE, length), F32)
        sum_1 = jnp.zeros((TILE, length), F32)
        sum_2 = jnp.zeros((TILE, length), F32)
        for y in range(TILE):
            rows = slice(y * TILE, (y + 1) * TILE)
            g = sw_s[rows] - before_s[rows] * ratio_s[rows]
            g_y = g * dy[y : y + 1]
            sum_0 = sum_0 + g
            sum_1 = sum_1 + g_y
            sum_2 = sum_2 + g_y * dy[y : y + 1]

        def total(value):
            return jnp.sum(value, axis=0, keepdims=True)

        m_x = sum_0 * dx
        m_0, m_10, m_20 = total(sum_0), total(m_x), total(m_x * dx)
        m_01, m_11, m_02 = total(sum_1), total(sum_1 * dx), total(sum_2)
        back = jnp.concatenate(
            [
                con_a * m_10 + con_b * m_01,
                con_b * m_10 + con_c * m_01,
                -0.5 * m_20,
                -m_11,
                -0.5 * m_02,
                grad_colour,
                m_0,
                jnp.zeros((ROWS - 9, length), F32),
            ],
            axis=0,
        )
        parts = jnp.concatenate(split(back, 2), axis=0)

        def scatter(c):
            at = pl.ds(aligned(c, CHUNK), CHUNK)
            both = mm_nt(parts, sel_s[at, :])
            grad_s[view, :, at] = grad_s[view, :, at] + both[0:ROWS] + both[ROWS:]

        loop(slots // CHUNK, scatter)

    loop(tiles, tile)

    def pack(b):
        swapped = swap_segments([grad_s[v, :, pl.ds(aligned(b, LANES), LANES)] for v in range(VIEWS)])
        for o in range(SEGS):
            back_ref[b * SEGS + o] = swapped[o]

    if owners <= 16:
        for b in range(owners // SEGS):
            pack(b)
    else:
        loop(owners // SEGS, pack)


def whole(shape):
    return pl.BlockSpec(shape, lambda i: (0,) * len(shape))


def local(
    centres, factor, harmonics, opacity, cameras, requests, tile_lists, tile_ids, image_cotangent
):
    gauss = centres.shape[1]
    slots = requests.shape[0]
    owners = slots // CAP
    tiles, length = tile_lists.shape
    chunks = slots // CHUNK
    params = pltpu.CompilerParams(vmem_limit_bytes=VMEM_LIMIT)
    wanted = lax.all_to_all(requests, "gs", split_axis=0, concat_axis=0, tiled=True).reshape(1, slots)

    want_spec = pl.BlockSpec((1, CHUNK), lambda i: (0, i))
    block_spec = pl.BlockSpec((CHUNK // CAP, ROWS, LANES), lambda i: (i, 0, 0))
    raw_spec = pl.BlockSpec((64, CHUNK), lambda i: (0, i))
    owned = [whole((3, gauss)), whole((9, gauss)), whole((48, gauss)), whole((1, gauss))]
    block_type = jax.ShapeDtypeStruct((owners, ROWS, LANES), F32)

    picked, raw = pl.pallas_call(
        project_kernel,
        grid=(chunks,),
        in_specs=[want_spec] + owned + [whole((VIEWS, 3))],
        out_specs=[block_spec, raw_spec],
        out_shape=[block_type, jax.ShapeDtypeStruct((64, slots), F32)],
        scratch_shapes=[pltpu.VMEM((192, gauss), BF16)],
        compiler_params=params,
    )(wanted, centres, factor, harmonics, opacity.reshape(1, gauss), cameras)
    records = lax.all_to_all(picked, "gs", split_axis=0, concat_axis=0, tiled=True)

    vmem = pl.BlockSpec(memory_space=pltpu.VMEM)
    image, back = pl.pallas_call(
        raster_kernel,
        in_specs=[pl.BlockSpec(memory_space=pltpu.SMEM), vmem, vmem, vmem],
        out_specs=[vmem, vmem],
        out_shape=[jax.ShapeDtypeStruct((3, tiles, PIX), F32), block_type],
        scratch_shapes=[
            pltpu.VMEM((VIEWS, 3 * ROWS, slots), BF16),
            pltpu.VMEM((slots, length), BF16),
            pltpu.VMEM((VIEWS, ROWS, slots), F32),
            pltpu.VMEM((2, PIX, length), BF16),
            pltpu.VMEM((PIX, length), F32),
            pltpu.VMEM((PIX, length), F32),
            pltpu.VMEM((PIX, length), F32),
            pltpu.VMEM((PIX, length), F32),
            pltpu.VMEM((2, PIX, length), BF16),
            pltpu.VMEM((PIX, length), F32),
            pltpu.VMEM((2, PIX, length), BF16),
        ],
        compiler_params=params,
    )(tile_ids, records, tile_lists, image_cotangent)
    returned = lax.all_to_all(back, "gs", split_axis=0, concat_axis=0, tiled=True)

    grads = pl.pallas_call(
        pull_kernel,
        grid=(chunks,),
        in_specs=[want_spec, block_spec, raw_spec, whole((VIEWS, 3))],
        out_specs=owned,
        out_shape=[jax.ShapeDtypeStruct((n, gauss), F32) for n in (3, 9, 48, 1)],
        compiler_params=params,
    )(wanted, returned, raw, cameras)
    return (image, grads[0], grads[1], grads[2], grads[3].reshape(gauss))


def solution(mesh):
    in_specs = (
        P(None, ("grp", "gs")),
        P(None, ("grp", "gs")),
        P(None, ("grp", "gs")),
        P(("grp", "gs")),
        P("grp", None),
        P(("grp", "gs")),
        P(("grp", "gs"), None),
        P(("grp", "gs")),
        P(None, ("grp", "gs"), None),
    )
    out_specs = (
        P(None, ("grp", "gs"), None),
        P(None, ("grp", "gs")),
        P(None, ("grp", "gs")),
        P(None, ("grp", "gs")),
        P(("grp", "gs")),
    )
    return jax.shard_map(local, mesh=mesh, in_specs=in_specs, out_specs=out_specs, check_vma=False)
```

profile of v0, /device:TPU:0, one launch (start us, length us, event | category | flops | bytes accessed | tf_op | source)
XLA Modules:
  0.0 58.7 jit_solution(13871312487235341567)
XLA Ops:
  0.6 0.8 %all_to_all.12 = s32[16,32,1]{1,2,0:T(1,128)S(1)} reshape(s32[512]{0:T(512)} %param.14) | data formatting | bytes 4096 | tf_op jit(solution)/shard_map/all_to_all | solution.py:417
  1.4 13.6 %all_to_all.19 = s32[16,32,1]{1,2,0:T(1,128)S(1)} all-to-all(s32[16,32,1]{1,2,0:T(1,128)S(1)} %all_to_all.12), channel_id=1, replica_groups=mesh['grp'=2,'gs'=16] {'gs'}, dimensions={0} | all-to-all | bytes 4096 | tf_op jit(solution)/shard_map/all_to_all | solution.py:417
  15.0 0.0 copy-start.4
  15.0 0.5 broadcast.3
  15.5 0.7 %reduce.3 = s32[16,32]{1,0:T(8,128)S(1)} reduce(s32[16,32,1]{1,2,0:T(1,128)S(1)} %all_to_all.19, s32[]{:T(128)} %broadcast.3), dimensions={2}, to_apply=%all_to_all.13.reduce_sub_computation.3 | reduce | bytes 4100 | tf_op jit(solution)/shard_map/all_to_all | solution.py:417
  16.2 0.0 copy-start.6
  16.2 0.1 reshape.22.want_ref
  16.3 0.0 copy-done.4
  16.3 0.6 %copy-done.6 = f32[4,3]{1,0:T(4,128)S(1)} copy-done((f32[4,3]{1,0:T(4,128)S(1)}, f32[4,3]{1,0:T(4,128)}, u32[]{:S(2)}) %copy-start.6) | copy-done | bytes 72
  16.9 0.0 copy-start
  16.9 1.1 %copy-done = f32[48,4096]{1,0:T(8,128)S(1)} copy-done((f32[48,4096]{1,0:T(8,128)S(1)}, f32[48,4096]{1,0:T(8,128)}, u32[]{:S(2)}) %copy-start) | copy-done | bytes 786456
  18.0 0.0 copy-start.1
  18.0 0.9 %copy-done.1 = f32[9,4096]{1,0:T(8,128)S(1)} copy-done((f32[9,4096]{1,0:T(8,128)S(1)}, f32[9,4096]{1,0:T(8,128)}, u32[]{:S(2)}) %copy-start.1) | copy-done | bytes 147480
  19.0 0.0 copy-start.2
  19.0 0.8 %copy-done.2 = f32[3,4096]{1,0:T(4,128)S(1)} copy-done((f32[3,4096]{1,0:T(4,128)S(1)}, f32[3,4096]{1,0:T(4,128)}, u32[]{:S(2)}) %copy-start.2) | copy-done | bytes 49176
  19.8 1.3 %shard_map.128 = (f32[16,16,128]{2,1,0:T(8,128)S(1)}, f32[64,512]{1,0:T(8,128)S(1)}) custom-call(s32[1,512]{1,0:T(1,128)S(1)} %reshape.22.want_ref, f32[3,4096]{1,0:T(4,128)S(1)} %copy-done.2, f32[9,4096]{1,0:T(8,128)S(1)} %copy-done.1, f32[48,4096]{1,0:T(8,128)S(1)} %copy-done, f32[1,4096]{1,0:T(1,128)S(1)} %bitcast.3, f32[4,3]{1,0:T(4,128)S(1)} %copy-done.6), custom_call_target="tpu_custom_call" | custom-call | tf_op jit(solution)/shard_map/pallas_call | solution.py:425
  21.1 0.0 copy-start.3
  21.1 0.0 copy-start.5
  21.1 0.0 copy-start.7
  21.1 10.7 %all_to_all.20.rec_ref = f32[16,16,128]{2,1,0:T(8,128)S(1)} all-to-all(f32[16,16,128]{2,1,0:T(8,128)S(1)} %get-tuple-element.13), channel_id=1, replica_groups=mesh['grp'=2,'gs'=16] {'gs'}, dimensions={0} | all-to-all | bytes 262144 | tf_op jit(solution)/shard_map/all_to_all | solution.py:434
  31.8 0.0 copy-done.3
  31.8 0.0 copy-done.5
  31.8 0.0 copy-done.7
  31.8 13.2 %shard_map.129 = (f32[3,8,256]{2,1,0:T(8,128)}, f32[16,16,128]{2,1,0:T(8,128)S(1)}) custom-call(s32[8]{0:T(128)S(1)} %copy-done.7, f32[16,16,128]{2,1,0:T(8,128)S(1)} %all_to_all.20.rec_ref, s32[8,512]{1,0:T(8,128)S(1)} %copy-done.5, f32[3,8,256]{2,1,0:T(8,128)S(1)} %copy-done.3), custom_call_target="tpu_custom_call" | custom-call | tf_op jit(solution)/shard_map/pallas_call | solution.py:437
  45.0 10.5 %all_to_all.21.back_ref = f32[16,16,128]{2,1,0:T(8,128)S(1)} all-to-all(f32[16,16,128]{2,1,0:T(8,128)S(1)} %get-tuple-element.15), channel_id=1, replica_groups=mesh['grp'=2,'gs'=16] {'gs'}, dimensions={0} | all-to-all | bytes 262144 | tf_op jit(solution)/shard_map/all_to_all | solution.py:457
  55.5 3.1 %shard_map.130 = (f32[3,4096]{1,0:T(4,128)}, f32[9,4096]{1,0:T(8,128)}, f32[48,4096]{1,0:T(8,128)}, f32[1,4096]{1,0:T(1,128)}) custom-call(s32[1,512]{1,0:T(1,128)S(1)} %reshape.22.want_ref, f32[16,16,128]{2,1,0:T(8,128)S(1)} %all_to_all.21.back_ref, f32[64,512]{1,0:T(8,128)S(1)} %get-tuple-element.16.raw_ref, f32[4,3]{1,0:T(4,128)S(1)} %copy-done.6), custom_call_target="tpu_custom_call" | custom-call | tf_op jit(solution)/shard_map/pallas_call | solution.py:459
Async XLA Ops:
  15.0 1.3 %copy-start.4 = (f32[4096]{0:T(1024)S(1)}, f32[4096]{0:T(1024)}, u32[]{:S(2)}) copy-start(f32[4096]{0:T(1024)} %param.12) | copy-start | bytes 49156
  16.2 0.7 %copy-start.6 = (f32[4,3]{1,0:T(4,128)S(1)}, f32[4,3]{1,0:T(4,128)}, u32[]{:S(2)}) copy-start(f32[4,3]{1,0:T(4,128)} %cam_ref.3) | copy-start | bytes 148
  16.9 1.1 %copy-start = (f32[48,4096]{1,0:T(8,128)S(1)}, f32[48,4096]{1,0:T(8,128)}, u32[]{:S(2)}) copy-start(f32[48,4096]{1,0:T(8,128)} %har_ref.1) | copy-start | bytes 2359300
  18.0 0.9 %copy-start.1 = (f32[9,4096]{1,0:T(8,128)S(1)}, f32[9,4096]{1,0:T(8,128)}, u32[]{:S(2)}) copy-start(f32[9,4096]{1,0:T(8,128)} %fac_ref.1) | copy-start | bytes 442372
  19.0 0.8 %copy-start.2 = (f32[3,4096]{1,0:T(4,128)S(1)}, f32[3,4096]{1,0:T(4,128)}, u32[]{:S(2)}) copy-start(f32[3,4096]{1,0:T(4,128)} %cen_ref.1) | copy-start | bytes 147460
  21.1 10.7 %copy-start.3 = (f32[3,8,256]{2,1,0:T(8,128)S(1)}, f32[3,8,256]{2,1,0:T(8,128)}, u32[]{:S(2)}) copy-start(f32[3,8,256]{2,1,0:T(8,128)} %cot_ref.1) | copy-start | bytes 73732
  21.1 10.7 %copy-start.5 = (s32[8,512]{1,0:T(8,128)S(1)}, s32[8,512]{1,0:T(8,128)}, u32[]{:S(2)}) copy-start(s32[8,512]{1,0:T(8,128)} %list_ref.1) | copy-start | bytes 49156
  21.1 10.7 %copy-start.7 = (s32[8]{0:T(128)S(1)}, s32[8]{0:T(128)}, u32[]{:S(2)}) copy-start(s32[8]{0:T(128)} %ids_ref.1) | copy-start | bytes 100
where the time goes:
time: 59.1 us; the launch traced here: 58.7 us
  blocking collectives  34.8 us (59%)
  Pallas kernels  17.7 us (30%)
  local copies, waits for them, and re-layouts  4.9 us (8%)
  between operations  0.69 us (1%)
  other arithmetic  0.67 us (1%)
    all_to_all x1, blocking collectives, local(): lax.all_to_all(requests, 'gs', split_axis=0, concat_axis=0, tiled=True)  13.6 us
    pallas_call x1, Pallas kernels, local(): pl.pallas_call(raster_kernel, in_specs=[pl.BlockSpec(memory_space=pltpu.S...  13.2 us
    all_to_all x1, blocking collectives, local(): lax.all_to_all(picked, 'gs', split_axis=0, concat_axis=0, tiled=True)  10.7 us
    all_to_all x1, blocking collectives, local(): lax.all_to_all(back, 'gs', split_axis=0, concat_axis=0, tiled=True)  10.5 us
    unnamed x16, local copies, waits for them, and re-layouts  3.54 us
    pallas_call x1, Pallas kernels, local(): pl.pallas_call(pull_kernel, grid=(chunks,), in_specs=[want_spec, block_sp...  3.13 us
    pallas_call x1, Pallas kernels, local(): pl.pallas_call(project_kernel, grid=(chunks,), in_specs=[want_spec] + own...  1.28 us
    all_to_all x2, local copies, waits for them, and re-layouts, local(): lax.all_to_all(requests, 'gs', split_axis=0, concat_axis=0, tiled=True)  1.28 us

commit v1 on v0

--- a/solution.py
+++ b/solution.py
@@ -148,35 +148,123 @@
     return [cam_ref[:, i : i + 1] for i in range(3)]
 
 
-def project_kernel(want_ref, cen_ref, fac_ref, har_ref, opa_ref, cam_ref, rec_ref, raw_ref, parts_ref):
+def partners(owners, body):
+    me = lax.axis_index("gs")
+
+    def step(i, carry):
+        body(lax.rem(me + i, owners))
+        return carry
+
+    lax.fori_loop(1, owners, step, 0, unroll=owners <= 16)
+
+
+def greet(owners):
+    barrier = pltpu.get_barrier_semaphore()
+    partners(owners, lambda p: pl.semaphore_signal(
+        barrier, inc=1, device_id={"gs": p}, device_id_type=pl.DeviceIdType.MESH))
+    return barrier
+
+
+def block_copy(source, target, send_sem, recv_sem, sender, partner):
+    return pltpu.make_async_remote_copy(
+        src_ref=source, dst_ref=target, send_sem=send_sem.at[partner], recv_sem=recv_sem.at[sender],
+        device_id={"gs": partner}, device_id_type=pl.DeviceIdType.MESH)
+
+
+def swap_blocks(owners, source, target, send_sem, recv_sem):
+    me = lax.axis_index("gs")
+    partners(owners, lambda p: block_copy(
+        source(p), target.at[me], send_sem, recv_sem, me, p).start())
+
+    def finish():
+        partners(owners, lambda p: block_copy(
+            source(p), target.at[p], send_sem, recv_sem, p, p).wait_recv())
+        partners(owners, lambda p: block_copy(
+            source(p), target.at[me], send_sem, recv_sem, me, p).wait_send())
+
+    return finish
+
+
+def project_kernel(
+    req_ref, cen_hbm, fac_hbm, har_hbm, opa_hbm, cam_ref, rec_ref, raw_ref, want_ref,
+    cen_ref, fac_ref, har_ref, opa_ref, parts_ref, got_ref, ask_ref, out_ref,
+    load_sem, ask_send, ask_recv, rec_send, rec_recv,
+):
+    owners = rec_ref.shape[0]
     gauss = cen_ref.shape[1]
+    me = lax.axis_index("gs")
+    loads = [
+        pltpu.make_async_copy(src, dst, load_sem.at[i])
+        for i, (src, dst) in enumerate(
+            [(cen_hbm, cen_ref), (fac_hbm, fac_ref), (har_hbm, har_ref), (opa_hbm, opa_ref)])
+    ]
+    for load in loads:
+        load.start()
+    barrier = greet(owners)
+    pl.semaphore_wait(barrier, owners - 1)
+    finish = swap_blocks(owners, lambda p: req_ref.at[p // SEGS], got_ref, ask_send, ask_recv)
+    got_ref[me] = req_ref[me // SEGS]
+    for load in loads:
+        load.wait()
     for base in range(0, gauss, CHUNK):
         cols = slice(base, base + CHUNK)
         whole = jnp.concatenate(
             [har_ref[:, cols], fac_ref[:, cols], cen_ref[:, cols], opa_ref[:, cols],
              jnp.zeros((3, CHUNK), F32)], axis=0)
         parts_ref[:, cols] = jnp.concatenate(split(whole, 3), axis=0)
-    want = jnp.maximum(want_ref[...], 0)
-    acc = jnp.zeros((192, CHUNK), F32)
-    for base in range(0, gauss, CHUNK):
-        acc = acc + mm(parts_ref[:, base : base + CHUNK], one_hot(base, want, CHUNK))
-    raw = acc[0:64] + acc[64:128] + acc[128:192]
-    raw_ref[...] = raw
-    pos, shape, coeffs, logit = raw_rows(raw)
-    records, basis = geometry(pos, shape, camera_columns(cam_ref))
-    for c in range(3):
-        summed = jnp.full_like(basis[0], 0.5)
-        for j in range(16):
-            summed = summed + basis[j] * coeffs[16 * c + j]
-        records.append(summed)
-    strength = 1.0 / (1.0 + jnp.exp(-logit))
-    records.append(jnp.broadcast_to(strength, (VIEWS, CHUNK)))
-    blank = jnp.zeros((ROWS - 9, CHUNK), F32)
-    by_view = [jnp.concatenate([r[v : v + 1] for r in records] + [blank], axis=0) for v in range(VIEWS)]
-    for b in range(CHUNK // LANES):
-        swapped = swap_segments([x[:, b * LANES : (b + 1) * LANES] for x in by_view])
-        for o in range(SEGS):
-            rec_ref[b * SEGS + o] = swapped[o]
+    finish()
+    seg = lax.broadcasted_iota(jnp.int32, (owners, LANES), 1) // CAP
+    row = lax.broadcasted_iota(jnp.int32, (owners, LANES), 0)
+    mine = jnp.where(seg == lax.rem(me, SEGS), got_ref[:, 0, :], 0)
+    spread = mine
+    for s in range(1, SEGS):
+        spread = spread + pltpu.roll(mine, CAP * s, 1)
+    ask_ref[...] = jnp.where(seg == lax.rem(row, SEGS), spread, 0)
+
+    def project(c):
+        near = ask_ref[pl.ds(aligned(c, CHUNK // CAP), CHUNK // CAP), :]
+        asked = jnp.concatenate(
+            [jnp.sum(near[b * SEGS : (b + 1) * SEGS], axis=0, keepdims=True)
+             for b in range(CHUNK // LANES)], axis=1)
+        lanes = pl.ds(aligned(c, CHUNK), CHUNK)
+        want_ref[:, lanes] = asked
+        want = jnp.maximum(asked, 0)
+        acc = jnp.zeros((192, CHUNK), F32)
+        for base in range(0, gauss, CHUNK):
+            acc = acc + mm(parts_ref[:, base : base + CHUNK], one_hot(base, want, CHUNK))
+        raw = acc[0:64] + acc[64:128] + acc[128:192]
+        raw_ref[:, lanes] = raw
+        pos, shape, coeffs, logit = raw_rows(raw)
+        records, basis = geometry(pos, shape, camera_columns(cam_ref))
+        for ch in range(3):
+            summed = jnp.full_like(basis[0], 0.5)
+            for j in range(16):
+                summed = summed + basis[j] * coeffs[16 * ch + j]
+            records.append(summed)
+        strength = 1.0 / (1.0 + jnp.exp(-logit))
+        records.append(jnp.broadcast_to(strength, (VIEWS, CHUNK)))
+        blank = jnp.zeros((ROWS - 9, CHUNK), F32)
+        by_view = [
+            jnp.concatenate([r[v : v + 1] for r in records] + [blank], axis=0) for v in range(VIEWS)]
+        for b in range(CHUNK // LANES):
+            swapped = swap_segments([x[:, b * LANES : (b + 1) * LANES] for x in by_view])
+            for o in range(SEGS):
+                out_ref[c * (CHUNK // CAP) + b * SEGS + o] = swapped[o]
+
+    loop(owners * CAP // CHUNK, project)
+    finish = swap_blocks(owners, lambda p: out_ref.at[p], rec_ref, rec_send, rec_recv)
+    rec_ref[me] = out_ref[me]
+    finish()
+
+
+def swap_kernel(in_ref, out_ref, send_sem, recv_sem):
+    owners = in_ref.shape[0]
+    me = lax.axis_index("gs")
+    barrier = greet(owners)
+    pl.semaphore_wait(barrier, owners - 1)
+    finish = swap_blocks(owners, lambda p: in_ref.at[p], out_ref, send_sem, recv_sem)
+    out_ref[me] = in_ref[me]
+    finish()
 
 
 def pull_kernel(want_ref, back_ref, raw_ref, cam_ref, cen_ref, fac_ref, har_ref, opa_ref):
@@ -414,26 +502,43 @@
     tiles, length = tile_lists.shape
     chunks = slots // CHUNK
     params = pltpu.CompilerParams(vmem_limit_bytes=VMEM_LIMIT)
-    wanted = lax.all_to_all(requests, "gs", split_axis=0, concat_axis=0, tiled=True).reshape(1, slots)
-
     want_spec = pl.BlockSpec((1, CHUNK), lambda i: (0, i))
     block_spec = pl.BlockSpec((CHUNK // CAP, ROWS, LANES), lambda i: (i, 0, 0))
     raw_spec = pl.BlockSpec((64, CHUNK), lambda i: (0, i))
     owned = [whole((3, gauss)), whole((9, gauss)), whole((48, gauss)), whole((1, gauss))]
     block_type = jax.ShapeDtypeStruct((owners, ROWS, LANES), F32)
 
-    picked, raw = pl.pallas_call(
+    vmem = pl.BlockSpec(memory_space=pltpu.VMEM)
+    hbm = pl.BlockSpec(memory_space=pltpu.HBM)
+    sems = pltpu.SemaphoreType.DMA((owners,))
+    records, raw, wanted = pl.pallas_call(
         project_kernel,
-        grid=(chunks,),
-        in_specs=[want_spec] + owned + [whole((VIEWS, 3))],
-        out_specs=[block_spec, raw_spec],
-        out_shape=[block_type, jax.ShapeDtypeStruct((64, slots), F32)],
-        scratch_shapes=[pltpu.VMEM((192, gauss), BF16)],
-        compiler_params=params,
-    )(wanted, centres, factor, harmonics, opacity.reshape(1, gauss), cameras)
-    records = lax.all_to_all(picked, "gs", split_axis=0, concat_axis=0, tiled=True)
-
-    vmem = pl.BlockSpec(memory_space=pltpu.VMEM)
+        in_specs=[vmem, hbm, hbm, hbm, hbm, vmem],
+        out_specs=[vmem, vmem, vmem],
+        out_shape=[
+            block_type,
+            jax.ShapeDtypeStruct((64, slots), F32),
+            jax.ShapeDtypeStruct((1, slots), jnp.int32),
+        ],
+        scratch_shapes=[
+            pltpu.VMEM((3, gauss), F32),
+            pltpu.VMEM((9, gauss), F32),
+            pltpu.VMEM((48, gauss), F32),
+            pltpu.VMEM((1, gauss), F32),
+            pltpu.VMEM((192, gauss), BF16),
+            pltpu.VMEM((owners, 1, LANES), jnp.int32),
+            pltpu.VMEM((owners, LANES), jnp.int32),
+            pltpu.VMEM((owners, ROWS, LANES), F32),
+            pltpu.SemaphoreType.DMA((4,)),
+            sems, sems, sems, sems,
+        ],
+        compiler_params=pltpu.CompilerParams(
+            vmem_limit_bytes=VMEM_LIMIT, collective_id=0, has_side_effects=True),
+    )(
+        requests.reshape(slots // LANES, 1, LANES), centres, factor, harmonics,
+        opacity.reshape(1, gauss), cameras,
+    )
+
     image, back = pl.pallas_call(
         raster_kernel,
         in_specs=[pl.BlockSpec(memory_space=pltpu.SMEM), vmem, vmem, vmem],
@@ -454,7 +559,14 @@
         ],
         compiler_params=params,
     )(tile_ids, records, tile_lists, image_cotangent)
-    returned = lax.all_to_all(back, "gs", split_axis=0, concat_axis=0, tiled=True)
+    returned = pl.pallas_call(
+        swap_kernel,
+        in_specs=[vmem],
+        out_specs=vmem,
+        out_shape=block_type,
+        scratch_shapes=[sems, sems],
+        compiler_params=pltpu.CompilerParams(collective_id=1, has_side_effects=True),
+    )(back)
 
     grads = pl.pallas_call(
         pull_kernel,

time: 59.1 us -> 49.2 us (0.83)
  blocking collectives: 34.8 us -> 0 us
  Pallas kernels: 17.7 us -> 40.9 us
  local copies, waits for them, and re-layouts: 4.9 us -> 7.18 us
  other arithmetic: 0.67 us -> 0 us
    all_to_all x3 -> x0, blocking collectives: 34.8 us -> none  [the longest x1 13.6 us: local(): lax.all_to_all(requests, 'gs', split_axis=0, concat_axis=0, tiled=True)]
    pallas_call x1 -> x2, Pallas kernels: 1.28 us -> 24.5 us  [the longest x1 16.2 us: local(): pl.pallas_call(project_kernel, in_specs=[vmem, hbm, hbm, hbm, hbm, vmem],...]
    unnamed x16 -> x22, local copies, waits for them, and re-layouts: 3.54 us -> 7.18 us
    all_to_all x2 -> x0, local copies, waits for them, and re-layouts: 1.28 us -> none  [local(): lax.all_to_all(requests, 'gs', split_axis=0, concat_axis=0, tiled=True)]
    all_to_all x1 -> x0, other arithmetic: 0.67 us -> none  [local(): lax.all_to_all(requests, 'gs', split_axis=0, concat_axis=0, tiled=True)]
where the time goes in v1:
time: 49.2 us; the launch traced here: 48.8 us
  Pallas kernels  40.9 us (83%)
  local copies, waits for them, and re-layouts  7.18 us (15%)
  between operations  0.7 us (1%)
    pallas_call x1, Pallas kernels, local(): pl.pallas_call(project_kernel, in_specs=[vmem, hbm, hbm, hbm, hbm, vmem],...  16.2 us
    pallas_call x1, Pallas kernels, local(): pl.pallas_call(raster_kernel, in_specs=[pl.BlockSpec(memory_space=pltpu.S...  13.2 us
    pallas_call x1, Pallas kernels, local(): pl.pallas_call(swap_kernel, in_specs=[vmem], out_specs=vmem, out_shape=bl...  8.34 us
    unnamed x22, local copies, waits for them, and re-layouts  7.18 us
    pallas_call x1, Pallas kernels, local(): pl.pallas_call(pull_kernel, grid=(chunks,), in_specs=[want_spec, block_sp...  3.13 us

profile of v1, /device:TPU:0, one launch (start us, length us, event | category | flops | bytes accessed | tf_op | source)
XLA Modules:
  0.0 48.8 jit_solution(11141237963411946826)
XLA Ops:
  0.6 0.0 copy-start.8
  0.6 0.7 %copy-done.8 = f32[4,3]{1,0:T(4,128)S(1)} copy-done((f32[4,3]{1,0:T(4,128)S(1)}, f32[4,3]{1,0:T(4,128)}, u32[]{:S(2)}) %copy-start.8) | copy-done | bytes 72
  1.3 0.0 copy-start
  1.3 1.1 %copy-done = f32[48,4096]{1,0:T(8,128)S(1)} copy-done((f32[48,4096]{1,0:T(8,128)S(1)}, f32[48,4096]{1,0:T(8,128)}, u32[]{:S(2)}) %copy-start) | copy-done | bytes 786456
  2.5 0.0 copy-start.2
  2.5 0.9 %copy-done.2 = f32[9,4096]{1,0:T(8,128)S(1)} copy-done((f32[9,4096]{1,0:T(8,128)S(1)}, f32[9,4096]{1,0:T(8,128)}, u32[]{:S(2)}) %copy-start.2) | copy-done | bytes 147480
  3.4 0.0 copy-start.4
  3.4 0.8 %copy-done.4 = f32[3,4096]{1,0:T(4,128)S(1)} copy-done((f32[3,4096]{1,0:T(4,128)S(1)}, f32[3,4096]{1,0:T(4,128)}, u32[]{:S(2)}) %copy-start.4) | copy-done | bytes 49176
  4.2 0.0 copy-start.6
  4.2 0.7 %copy-done.6 = f32[4096]{0:T(1024)S(1)} copy-done((f32[4096]{0:T(1024)S(1)}, f32[4096]{0:T(1024)}, u32[]{:S(2)}) %copy-start.6) | copy-done | bytes 16408
  5.0 0.0 copy-start.9
  5.0 0.7 %copy-done.9 = s32[512]{0:T(512)S(1)} copy-done((s32[512]{0:T(512)S(1)}, s32[512]{0:T(512)}, u32[]{:S(2)}) %copy-start.9) | copy-done | bytes 2072
  5.6 0.0 copy-start.5
  5.6 0.0 copy-start.7
  5.6 16.2 %shard_map.128 = (f32[16,16,128]{2,1,0:T(8,128)S(1)}, f32[64,512]{1,0:T(8,128)S(1)}, s32[1,512]{1,0:T(1,128)S(1)}) custom-call(s32[4,1,128]{2,1,0:T(1,128)S(1)} %bitcast.4, f32[3,4096]{1,0:T(4,128)S(1)} %copy-done.4, f32[9,4096]{1,0:T(8,128)S(1)} %copy-done.2, f32[48,4096]{1,0:T(8,128)S(1)} %copy-done, f32[1,4096]{1,0:T(1,128)S(1)} %bitcast.3, ...), custom_call_target="tpu_custom_call" | custom-call | tf_op jit(solution)/shard_map/pallas_call | solution.py:514
  21.9 0.0 copy-start.10
  21.9 0.0 copy-done.5
  21.9 0.0 copy-done.7
  21.9 0.6 %copy-done.10 = s32[8]{0:T(128)S(1)} copy-done((s32[8]{0:T(128)S(1)}, s32[8]{0:T(128)}, u32[]{:S(2)}) %copy-start.10) | copy-done | bytes 56
  22.5 13.2 %shard_map.129 = (f32[3,8,256]{2,1,0:T(8,128)}, f32[16,16,128]{2,1,0:T(8,128)S(1)}) custom-call(s32[8]{0:T(128)S(1)} %copy-done.10, f32[16,16,128]{2,1,0:T(8,128)S(1)} %get-tuple-element.14.rec_ref, s32[8,512]{1,0:T(8,128)S(1)} %copy-done.7, f32[3,8,256]{2,1,0:T(8,128)S(1)} %copy-done.5), custom_call_target="tpu_custom_call" | custom-call | tf_op jit(solution)/shard_map/pallas_call | solution.py:542
  35.8 0.0 copy-start.3
  35.8 0.7 %copy-done.3 = f32[16,16,128]{2,1,0:T(8,128)} copy-done((f32[16,16,128]{2,1,0:T(8,128)}, f32[16,16,128]{2,1,0:T(8,128)S(1)}, u32[]{:S(2)}) %copy-start.3) | copy-done | bytes 131096
  36.4 8.3 %shard_map.130.back_ref = f32[16,16,128]{2,1,0:T(8,128)} custom-call(f32[16,16,128]{2,1,0:T(8,128)} %copy-done.3), custom_call_target="tpu_custom_call" | custom-call | tf_op jit(solution)/shard_map/pallas_call | solution.py:562
  44.8 0.0 copy-start.1
  44.8 0.9 %copy-done.1 = f32[16,16,128]{2,1,0:T(8,128)S(1)} copy-done((f32[16,16,128]{2,1,0:T(8,128)S(1)}, f32[16,16,128]{2,1,0:T(8,128)}, u32[]{:S(2)}) %copy-start.1) | copy-done | bytes 131096
  45.7 3.1 %shard_map.131 = (f32[3,4096]{1,0:T(4,128)}, f32[9,4096]{1,0:T(8,128)}, f32[48,4096]{1,0:T(8,128)}, f32[1,4096]{1,0:T(1,128)}) custom-call(s32[1,512]{1,0:T(1,128)S(1)} %get-tuple-element.16.want_ref, f32[16,16,128]{2,1,0:T(8,128)S(1)} %copy-done.1, f32[64,512]{1,0:T(8,128)S(1)} %get-tuple-element.18.raw_ref, f32[4,3]{1,0:T(4,128)S(1)} %copy-done.8), custom_call_target="tpu_custom_call" | custom-call | tf_op jit(solution)/shard_map/pallas_call | solution.py:571
Async XLA Ops:
  0.6 0.7 %copy-start.8 = (f32[4,3]{1,0:T(4,128)S(1)}, f32[4,3]{1,0:T(4,128)}, u32[]{:S(2)}) copy-start(f32[4,3]{1,0:T(4,128)} %cam_ref.3) | copy-start | bytes 148
  1.3 1.1 %copy-start = (f32[48,4096]{1,0:T(8,128)S(1)}, f32[48,4096]{1,0:T(8,128)}, u32[]{:S(2)}) copy-start(f32[48,4096]{1,0:T(8,128)} %har_hbm.1) | copy-start | bytes 2359300
  2.5 0.9 %copy-start.2 = (f32[9,4096]{1,0:T(8,128)S(1)}, f32[9,4096]{1,0:T(8,128)}, u32[]{:S(2)}) copy-start(f32[9,4096]{1,0:T(8,128)} %fac_hbm.1) | copy-start | bytes 442372
  3.4 0.8 %copy-start.4 = (f32[3,4096]{1,0:T(4,128)S(1)}, f32[3,4096]{1,0:T(4,128)}, u32[]{:S(2)}) copy-start(f32[3,4096]{1,0:T(4,128)} %cen_hbm.1) | copy-start | bytes 147460
  4.2 0.7 %copy-start.6 = (f32[4096]{0:T(1024)S(1)}, f32[4096]{0:T(1024)}, u32[]{:S(2)}) copy-start(f32[4096]{0:T(1024)} %param.12) | copy-start | bytes 49156
  5.0 0.7 %copy-start.9 = (s32[512]{0:T(512)S(1)}, s32[512]{0:T(512)}, u32[]{:S(2)}) copy-start(s32[512]{0:T(512)} %param.14) | copy-start | bytes 6148
  5.6 16.2 %copy-start.5 = (f32[3,8,256]{2,1,0:T(8,128)S(1)}, f32[3,8,256]{2,1,0:T(8,128)}, u32[]{:S(2)}) copy-start(f32[3,8,256]{2,1,0:T(8,128)} %cot_ref.1) | copy-start | bytes 73732
  5.6 16.2 %copy-start.7 = (s32[8,512]{1,0:T(8,128)S(1)}, s32[8,512]{1,0:T(8,128)}, u32[]{:S(2)}) copy-start(s32[8,512]{1,0:T(8,128)} %list_ref.1) | copy-start | bytes 49156
  21.9 0.7 %copy-start.10 = (s32[8]{0:T(128)S(1)}, s32[8]{0:T(128)}, u32[]{:S(2)}) copy-start(s32[8]{0:T(128)} %ids_ref.1) | copy-start | bytes 100
  35.8 0.7 %copy-start.3 = (f32[16,16,128]{2,1,0:T(8,128)}, f32[16,16,128]{2,1,0:T(8,128)S(1)}, u32[]{:S(2)}) copy-start(f32[16,16,128]{2,1,0:T(8,128)S(1)} %get-tuple-element.17.in_ref) | copy-start | bytes 393220
  44.8 0.9 %copy-start.1 = (f32[16,16,128]{2,1,0:T(8,128)S(1)}, f32[16,16,128]{2,1,0:T(8,128)}, u32[]{:S(2)}) copy-start(f32[16,16,128]{2,1,0:T(8,128)} %shard_map.130.back_ref) | copy-start | bytes 393220

commit v2 on v1

--- a/solution.py
+++ b/solution.py
@@ -22,7 +22,8 @@
 CHUNK = 512
 F32 = jnp.float32
 BF16 = jnp.bfloat16
-VMEM_LIMIT = 48 * 1024 * 1024
+VMEM_LIMIT = 60 * 1024 * 1024
+FIELDS = 9
 
 BAND_ONE = 0.4886025119029199
 
@@ -185,26 +186,32 @@
     return finish
 
 
-def project_kernel(
-    req_ref, cen_hbm, fac_hbm, har_hbm, opa_hbm, cam_ref, rec_ref, raw_ref, want_ref,
-    cen_ref, fac_ref, har_ref, opa_ref, parts_ref, got_ref, ask_ref, out_ref,
-    load_sem, ask_send, ask_recv, rec_send, rec_recv,
+def splat_kernel(
+    req_hbm, cen_hbm, fac_hbm, har_hbm, opa_hbm, cam_hbm, ids_hbm, list_hbm, cot_hbm,
+    img_ref, back_ref, raw_ref, want_ref,
+    req_ref, cen_ref, fac_ref, har_ref, opa_ref, cam_ref, ids_ref, list_ref, cot_ref,
+    parts_ref, got_ref, ask_ref, out_ref, rec_ref,
+    rec_s, sel_s, grad_s, lk_s, alpha_s, ratio_s, shade_s, before_s, w_s, sw_s, swp_s,
+    load_sem, ask_send, ask_recv, rec_send, rec_recv, back_send, back_recv,
 ):
     owners = rec_ref.shape[0]
     gauss = cen_ref.shape[1]
     me = lax.axis_index("gs")
     loads = [
         pltpu.make_async_copy(src, dst, load_sem.at[i])
-        for i, (src, dst) in enumerate(
-            [(cen_hbm, cen_ref), (fac_hbm, fac_ref), (har_hbm, har_ref), (opa_hbm, opa_ref)])
+        for i, (src, dst) in enumerate([
+            (req_hbm, req_ref), (har_hbm, har_ref), (fac_hbm, fac_ref), (cen_hbm, cen_ref),
+            (opa_hbm, opa_ref), (cam_hbm, cam_ref), (ids_hbm, ids_ref), (list_hbm, list_ref),
+            (cot_hbm, cot_ref)])
     ]
     for load in loads:
         load.start()
     barrier = greet(owners)
+    loads[0].wait()
     pl.semaphore_wait(barrier, owners - 1)
     finish = swap_blocks(owners, lambda p: req_ref.at[p // SEGS], got_ref, ask_send, ask_recv)
     got_ref[me] = req_ref[me // SEGS]
-    for load in loads:
+    for load in loads[1:]:
         load.wait()
     for base in range(0, gauss, CHUNK):
         cols = slice(base, base + CHUNK)
@@ -249,26 +256,24 @@
         for b in range(CHUNK // LANES):
             swapped = swap_segments([x[:, b * LANES : (b + 1) * LANES] for x in by_view])
             for o in range(SEGS):
-                out_ref[c * (CHUNK // CAP) + b * SEGS + o] = swapped[o]
+                out_ref[c * (CHUNK // CAP) + b * SEGS + o] = swapped[o][0:FIELDS]
 
     loop(owners * CAP // CHUNK, project)
     finish = swap_blocks(owners, lambda p: out_ref.at[p], rec_ref, rec_send, rec_recv)
     rec_ref[me] = out_ref[me]
     finish()
-
-
-def swap_kernel(in_ref, out_ref, send_sem, recv_sem):
-    owners = in_ref.shape[0]
-    me = lax.axis_index("gs")
-    barrier = greet(owners)
-    pl.semaphore_wait(barrier, owners - 1)
-    finish = swap_blocks(owners, lambda p: in_ref.at[p], out_ref, send_sem, recv_sem)
-    out_ref[me] = in_ref[me]
+    raster(
+        ids_ref, rec_ref, list_ref, cot_ref, img_ref, out_ref,
+        rec_s, sel_s, grad_s, lk_s, alpha_s, ratio_s, shade_s, before_s, w_s, sw_s, swp_s,
+    )
+    finish = swap_blocks(owners, lambda p: out_ref.at[p], back_ref, back_send, back_recv)
+    back_ref[me] = out_ref[me]
     finish()
 
 
-def pull_kernel(want_ref, back_ref, raw_ref, cam_ref, cen_ref, fac_ref, har_ref, opa_ref):
+def pull_kernel(want_ref, back_ref, raw_ref, cam_ref, img_ref, cen_ref, fac_ref, har_ref, opa_ref, out_ref):
     gauss = cen_ref.shape[1]
+    out_ref[...] = img_ref[...]
     by_view = [[] for _ in range(VIEWS)]
     for b in range(CHUNK // LANES):
         swapped = swap_segments([back_ref[b * SEGS + o] for o in range(SEGS)])
@@ -330,7 +335,7 @@
     return i * size if isinstance(i, int) else pl.multiple_of(i * size, size)
 
 
-def raster_kernel(
+def raster(
     ids_ref, rec_ref, list_ref, cot_ref, img_ref, back_ref,
     rec_s, sel_s, grad_s, lk_s, alpha_s, ratio_s, shade_s, before_s, w_s, sw_s, swp_s,
 ):
@@ -338,11 +343,13 @@
     slots = owners * CAP
     tiles, length = list_ref.shape
     half = length // 2
+    blank = jnp.zeros((ROWS - FIELDS, LANES), F32)
 
     def unpack(b):
         swapped = swap_segments([rec_ref[b * SEGS + o] for o in range(SEGS)])
         for v in range(VIEWS):
-            rec_s[v, :, pl.ds(aligned(b, LANES), LANES)] = jnp.concatenate(split(swapped[v], 3), axis=0)
+            rec_s[v, :, pl.ds(aligned(b, LANES), LANES)] = jnp.concatenate(
+                split(jnp.concatenate([swapped[v], blank], axis=0), 3), axis=0)
 
     if owners <= 16:
         for b in range(owners // SEGS):
@@ -471,7 +478,9 @@
         def scatter(c):
             at = pl.ds(aligned(c, CHUNK), CHUNK)
             both = mm_nt(parts, sel_s[at, :])
-            grad_s[view, :, at] = grad_s[view, :, at] + both[0:ROWS] + both[ROWS:]
+            added = both[0:ROWS] + both[ROWS:]
+            for v in range(VIEWS):
+                grad_s[v, :, at] = grad_s[v, :, at] + jnp.where(view == v, added, 0.0)
 
         loop(slots // CHUNK, scatter)
 
@@ -480,7 +489,7 @@
     def pack(b):
         swapped = swap_segments([grad_s[v, :, pl.ds(aligned(b, LANES), LANES)] for v in range(VIEWS)])
         for o in range(SEGS):
-            back_ref[b * SEGS + o] = swapped[o]
+            back_ref[b * SEGS + o] = swapped[o][0:FIELDS]
 
     if owners <= 16:
         for b in range(owners // SEGS):
@@ -503,80 +512,65 @@
     chunks = slots // CHUNK
     params = pltpu.CompilerParams(vmem_limit_bytes=VMEM_LIMIT)
     want_spec = pl.BlockSpec((1, CHUNK), lambda i: (0, i))
-    block_spec = pl.BlockSpec((CHUNK // CAP, ROWS, LANES), lambda i: (i, 0, 0))
+    block_spec = pl.BlockSpec((CHUNK // CAP, FIELDS, LANES), lambda i: (i, 0, 0))
     raw_spec = pl.BlockSpec((64, CHUNK), lambda i: (0, i))
     owned = [whole((3, gauss)), whole((9, gauss)), whole((48, gauss)), whole((1, gauss))]
-    block_type = jax.ShapeDtypeStruct((owners, ROWS, LANES), F32)
+    block_type = jax.ShapeDtypeStruct((owners, FIELDS, LANES), F32)
 
     vmem = pl.BlockSpec(memory_space=pltpu.VMEM)
-    hbm = pl.BlockSpec(memory_space=pltpu.HBM)
     sems = pltpu.SemaphoreType.DMA((owners,))
-    records, raw, wanted = pl.pallas_call(
-        project_kernel,
-        in_specs=[vmem, hbm, hbm, hbm, hbm, vmem],
-        out_specs=[vmem, vmem, vmem],
+    blocks = pltpu.VMEM((owners, FIELDS, LANES), F32)
+    plane = pltpu.VMEM((PIX, length), F32)
+    pair = pltpu.VMEM((2, PIX, length), BF16)
+    image_type = jax.ShapeDtypeStruct((3, tiles, PIX), F32)
+    image, returned, raw, wanted = pl.pallas_call(
+        splat_kernel,
+        in_specs=[pl.BlockSpec(memory_space=pl.ANY)] * 9,
+        out_specs=[vmem] * 4,
         out_shape=[
+            image_type,
             block_type,
             jax.ShapeDtypeStruct((64, slots), F32),
             jax.ShapeDtypeStruct((1, slots), jnp.int32),
         ],
         scratch_shapes=[
+            pltpu.VMEM((slots // LANES, 1, LANES), jnp.int32),
             pltpu.VMEM((3, gauss), F32),
             pltpu.VMEM((9, gauss), F32),
             pltpu.VMEM((48, gauss), F32),
             pltpu.VMEM((1, gauss), F32),
+            pltpu.VMEM((VIEWS, 3), F32),
+            pltpu.SMEM((tiles,), jnp.int32),
+            pltpu.VMEM((tiles, length), jnp.int32),
+            pltpu.VMEM((3, tiles, PIX), F32),
             pltpu.VMEM((192, gauss), BF16),
             pltpu.VMEM((owners, 1, LANES), jnp.int32),
             pltpu.VMEM((owners, LANES), jnp.int32),
-            pltpu.VMEM((owners, ROWS, LANES), F32),
-            pltpu.SemaphoreType.DMA((4,)),
-            sems, sems, sems, sems,
+            blocks,
+            blocks,
+            pltpu.VMEM((VIEWS, 3 * ROWS, slots), BF16),
+            pltpu.VMEM((slots, length), BF16),
+            pltpu.VMEM((VIEWS, ROWS, slots), F32),
+            pair, plane, plane, plane, plane, pair, plane, pair,
+            pltpu.SemaphoreType.DMA((9,)),
+            sems, sems, sems, sems, sems, sems,
         ],
         compiler_params=pltpu.CompilerParams(
             vmem_limit_bytes=VMEM_LIMIT, collective_id=0, has_side_effects=True),
     )(
         requests.reshape(slots // LANES, 1, LANES), centres, factor, harmonics,
-        opacity.reshape(1, gauss), cameras,
-    )
-
-    image, back = pl.pallas_call(
-        raster_kernel,
-        in_specs=[pl.BlockSpec(memory_space=pltpu.SMEM), vmem, vmem, vmem],
-        out_specs=[vmem, vmem],
-        out_shape=[jax.ShapeDtypeStruct((3, tiles, PIX), F32), block_type],
-        scratch_shapes=[
-            pltpu.VMEM((VIEWS, 3 * ROWS, slots), BF16),
-            pltpu.VMEM((slots, length), BF16),
-            pltpu.VMEM((VIEWS, ROWS, slots), F32),
-            pltpu.VMEM((2, PIX, length), BF16),
-            pltpu.VMEM((PIX, length), F32),
-            pltpu.VMEM((PIX, length), F32),
-            pltpu.VMEM((PIX, length), F32),
-            pltpu.VMEM((PIX, length), F32),
-            pltpu.VMEM((2, PIX, length), BF16),
-            pltpu.VMEM((PIX, length), F32),
-            pltpu.VMEM((2, PIX, length), BF16),
-        ],
-        compiler_params=params,
-    )(tile_ids, records, tile_lists, image_cotangent)
-    returned = pl.pallas_call(
-        swap_kernel,
-        in_specs=[vmem],
-        out_specs=vmem,
-        out_shape=block_type,
-        scratch_shapes=[sems, sems],
-        compiler_params=pltpu.CompilerParams(collective_id=1, has_side_effects=True),
-    )(back)
+        opacity.reshape(1, gauss), cameras, tile_ids, tile_lists, image_cotangent,
+    )
 
     grads = pl.pallas_call(
         pull_kernel,
         grid=(chunks,),
-        in_specs=[want_spec, block_spec, raw_spec, whole((VIEWS, 3))],
-        out_specs=owned,
-        out_shape=[jax.ShapeDtypeStruct((n, gauss), F32) for n in (3, 9, 48, 1)],
+        in_specs=[want_spec, block_spec, raw_spec, whole((VIEWS, 3)), whole((3, tiles, PIX))],
+        out_specs=owned + [whole((3, tiles, PIX))],
+        out_shape=[jax.ShapeDtypeStruct((n, gauss), F32) for n in (3, 9, 48, 1)] + [image_type],
         compiler_params=params,
-    )(wanted, returned, raw, cameras)
-    return (image, grads[0], grads[1], grads[2], grads[3].reshape(gauss))
+    )(wanted, returned, raw, cameras, image)
+    return (grads[4], grads[0], grads[1], grads[2], grads[3].reshape(gauss))
 
 
 def solution(mesh):

time: 49.2 us -> 37.4 us (0.76)
  local copies, waits for them, and re-layouts: 7.18 us -> 0 us
  Pallas kernels: 40.9 us -> 36.6 us
    unnamed x22 -> x0, local copies, waits for them, and re-layouts: 7.18 us -> none
    pallas_call x3 -> x1, Pallas kernels: 37.8 us -> 32.4 us  [local(): pl.pallas_call(splat_kernel, in_specs=[pl.BlockSpec(memory_space=pl.ANY)]...]
    pallas_call x1, Pallas kernels: 3.13 us -> 4.13 us  [local(): pl.pallas_call(pull_kernel, grid=(chunks,), in_specs=[want_spec, block_sp...]
where the time goes in v2:
time: 37.4 us; the launch traced here: 37.2 us
  Pallas kernels  36.6 us (98%)
  between operations  0.64 us (2%)
    pallas_call x1, Pallas kernels, local(): pl.pallas_call(splat_kernel, in_specs=[pl.BlockSpec(memory_space=pl.ANY)]...  32.4 us
    pallas_call x1, Pallas kernels, local(): pl.pallas_call(pull_kernel, grid=(chunks,), in_specs=[want_spec, block_sp...  4.13 us

profile of v2, /device:TPU:0, one launch (start us, length us, event | category | flops | bytes accessed | tf_op | source)
XLA Modules:
  0.0 37.2 jit_solution(8292548287757660063)
XLA Ops:
  0.6 32.4 %shard_map.128 = (f32[3,8,256]{2,1,0:T(8,128)}, f32[16,9,128]{2,1,0:T(8,128)}, f32[64,512]{1,0:T(8,128)}, s32[1,512]{1,0:T(1,128)}) custom-call(s32[4,1,128]{2,1,0:T(1,128)} %bitcast.4, f32[3,4096]{1,0:T(4,128)} %cen_hbm.1, f32[9,4096]{1,0:T(8,128)} %fac_hbm.1, f32[48,4096]{1,0:T(8,128)} %har_hbm.1, f32[1,4096]{1,0:T(1,128)} %bitcast.3, f32[4,3]{1,0:T(4,128)} %cam_ref.1, ...), custom_call_target="tpu_custom_call" | custom-call | tf_op jit(solution)/shard_map/pallas_call | solution.py:526
  33.1 4.1 %shard_map.129 = (f32[3,4096]{1,0:T(4,128)}, f32[9,4096]{1,0:T(8,128)}, f32[48,4096]{1,0:T(8,128)}, f32[1,4096]{1,0:T(1,128)}, f32[3,8,256]{2,1,0:T(8,128)}) custom-call(s32[1,512]{1,0:T(1,128)} %get-tuple-element.14.want_ref, f32[16,9,128]{2,1,0:T(8,128)} %get-tuple-element.15.back_ref, f32[64,512]{1,0:T(8,128)} %get-tuple-element.16.raw_ref, ...), custom_call_target="tpu_custom_call" | custom-call | tf_op jit(solution)/shard_map/pallas_call | solution.py:565

commit v3 on v2

--- a/solution.py
+++ b/solution.py
@@ -24,6 +24,8 @@
 BF16 = jnp.bfloat16
 VMEM_LIMIT = 60 * 1024 * 1024
 FIELDS = 9
+PAIR = 2
+LOG2E = 1.4426950408889634
 
 BAND_ONE = 0.4886025119029199
 
@@ -261,6 +263,15 @@
     loop(owners * CAP // CHUNK, project)
     finish = swap_blocks(owners, lambda p: out_ref.at[p], rec_ref, rec_send, rec_recv)
     rec_ref[me] = out_ref[me]
+
+    def selectors(t):
+        def part(c):
+            at = pl.ds(aligned(c, CHUNK), CHUNK)
+            sel_s[t, at, :] = one_hot(c * CHUNK, list_ref[pl.ds(t, 1), :], CHUNK)
+
+        loop(owners * CAP // CHUNK, part)
+
+    loop(list_ref.shape[0], selectors)
     finish()
     raster(
         ids_ref, rec_ref, list_ref, cot_ref, img_ref, out_ref,
@@ -364,21 +375,17 @@
     lower = jnp.where(row_i > col_i, 1.0, 0.0).astype(BF16)
     px = lax.broadcasted_iota(jnp.int32, (TILE, length), 0).astype(F32) + 0.5
 
-    def tile(t):
+    def tile(t, slot):
         code = ids_ref[t]
         view = code // (TILES_ACROSS * TILE_ROWS)
         place = code - view * (TILES_ACROSS * TILE_ROWS)
         line = place // TILES_ACROSS
         corner_y = (line * TILE).astype(F32)
         corner_x = ((place - line * TILES_ACROSS) * TILE).astype(F32)
-        entries = list_ref[pl.ds(t, 1), :]
-        got = [jnp.zeros((3 * ROWS, length), F32)]
 
         def gather(c):
             at = pl.ds(aligned(c, CHUNK), CHUNK)
-            sel = one_hot(c * CHUNK, entries, CHUNK)
-            sel_s[at, :] = sel
-            return mm(rec_s[view, :, at], sel)
+            return mm(rec_s[view, :, at], sel_s[t, at, :])
 
         if slots == CHUNK:
             got = gather(0)
@@ -391,68 +398,75 @@
         strength = rec[8:9]
         dx = (corner_x + px) - rec[0:1]
         dy = (corner_y + px) - rec[1:2]
-        quad_x = (-0.5 * con_a) * dx * dx
-        cross = (-con_b) * dx
-        quad_y = (-0.5 * con_c) * dy * dy
+        quad_x = (-0.5 * LOG2E * con_a) * dx * dx
+        cross = (-LOG2E * con_b) * dx
+        quad_y = (-0.5 * LOG2E * con_c) * dy * dy
+        yield
         for y in range(TILE):
             rows = slice(y * TILE, (y + 1) * TILE)
-            falloff = jnp.exp(quad_x + cross * dy[y : y + 1] + quad_y[y : y + 1])
+            falloff = jnp.exp2(quad_x + cross * dy[y : y + 1] + quad_y[y : y + 1])
             alpha = strength * falloff
-            keep = jnp.log(1.0 - alpha)
-            alpha_s[rows] = alpha
-            ratio_s[rows] = alpha * jnp.exp(-keep)
+            keep = jnp.log(1.0 - alpha) * LOG2E
+            alpha_s[slot, rows] = alpha
+            ratio_s[slot, rows] = alpha * jnp.exp2(-keep)
             hi, lo = split(keep, 2)
-            lk_s[0, rows] = hi
-            lk_s[1, rows] = lo
-        before_s[:, :half] = mm(lk_s[0, :, :half], upper[:half, :half]) + mm(
-            lk_s[1, :, :half], upper[:half, :half])
-        before_s[:, half:] = mm(lk_s[0], upper[:, half:]) + mm(lk_s[1], upper[:, half:])
+            lk_s[slot, 0, rows] = hi
+            lk_s[slot, 1, rows] = lo
+        yield
+        before_s[slot, :, :half] = mm(lk_s[slot, 0, :, :half], upper[:half, :half]) + mm(
+            lk_s[slot, 1, :, :half], upper[:half, :half])
+        before_s[slot, :, half:] = mm(lk_s[slot, 0], upper[:, half:]) + mm(lk_s[slot, 1], upper[:, half:])
 
         cot = jnp.concatenate([cot_ref[c, pl.ds(t, 1), :] for c in range(3)], axis=0)
         cot_hi, cot_lo = split(cot, 2)
         col_hi, col_lo = split(colour, 2)
         pad = jnp.zeros((ROWS - 9, PIX), BF16)
-        shade_s[...] = mm_tn(
+        shade_s[slot] = mm_tn(
             jnp.concatenate([cot_hi, cot_hi, cot_lo, pad], axis=0),
             jnp.concatenate([col_hi, col_lo, col_hi, jnp.zeros((ROWS - 9, length), BF16)], axis=0),
         )
+        yield
         for y in range(TILE):
             rows = slice(y * TILE, (y + 1) * TILE)
-            weight = alpha_s[rows] * jnp.exp(before_s[rows])
+            weight = alpha_s[slot, rows] * jnp.exp2(before_s[slot, rows])
             hi, lo = split(weight, 2)
-            w_s[0, rows] = hi
-            w_s[1, rows] = lo
-            shaded = shade_s[rows] * weight
-            sw_s[rows] = shaded
+            w_s[slot, 0, rows] = hi
+            w_s[slot, 1, rows] = lo
+            shaded = shade_s[slot, rows] * weight
+            sw_s[slot, rows] = shaded
             hi, lo = split(shaded, 2)
-            swp_s[0, rows] = hi
-            swp_s[1, rows] = lo
-        before_s[:, half:] = mm(swp_s[0, :, half:], lower[half:, half:]) + mm(
-            swp_s[1, :, half:], lower[half:, half:])
-        before_s[:, :half] = mm(swp_s[0], lower[:, :half]) + mm(swp_s[1], lower[:, :half])
+            swp_s[slot, 0, rows] = hi
+            swp_s[slot, 1, rows] = lo
+        yield
+        before_s[slot, :, half:] = mm(swp_s[slot, 0, :, half:], lower[half:, half:]) + mm(
+            swp_s[slot, 1, :, half:], lower[half:, half:])
+        before_s[slot, :, :half] = mm(swp_s[slot, 0], lower[:, :half]) + mm(swp_s[slot, 1], lower[:, :half])
 
         six = jnp.zeros((2, length), BF16)
         col_parts = jnp.concatenate([col_hi, col_lo, six], axis=0)
-        by_hi = mm_nt(col_parts, w_s[0])
-        by_lo = mm_nt(col_parts, w_s[1])
+        by_hi = mm_nt(col_parts, w_s[slot, 0])
+        by_lo = mm_nt(col_parts, w_s[slot, 1])
         image = by_hi[0:3] + by_hi[3:6] + by_lo[0:3]
         for c in range(3):
             img_ref[c, pl.ds(t, 1), :] = image[c : c + 1]
         cot_parts = jnp.concatenate([cot_hi, cot_lo, jnp.zeros((2, PIX), BF16)], axis=0)
-        by_hi = mm(cot_parts, w_s[0])
-        by_lo = mm(cot_parts, w_s[1])
+        by_hi = mm(cot_parts, w_s[slot, 0])
+        by_lo = mm(cot_parts, w_s[slot, 1])
         grad_colour = by_hi[0:3] + by_hi[3:6] + by_lo[0:3]
 
         sum_0 = jnp.zeros((TILE, length), F32)
         sum_1 = jnp.zeros((TILE, length), F32)
         sum_2 = jnp.zeros((TILE, length), F32)
+        yield
         for y in range(TILE):
             rows = slice(y * TILE, (y + 1) * TILE)
-            g = sw_s[rows] - before_s[rows] * ratio_s[rows]
+            g = sw_s[slot, rows] - before_s[slot, rows] * ratio_s[slot, rows]
             g_y = g * dy[y : y + 1]
             sum_0 = sum_0 + g
             sum_1 = sum_1 + g_y
             sum_2 = sum_2 + g_y * dy[y : y + 1]
+
+        yield
 
         def total(value):
             return jnp.sum(value, axis=0, keepdims=True)
@@ -477,14 +491,19 @@
 
         def scatter(c):
             at = pl.ds(aligned(c, CHUNK), CHUNK)
-            both = mm_nt(parts, sel_s[at, :])
+            both = mm_nt(parts, sel_s[t, at, :])
             added = both[0:ROWS] + both[ROWS:]
             for v in range(VIEWS):
                 grad_s[v, :, at] = grad_s[v, :, at] + jnp.where(view == v, added, 0.0)
 
         loop(slots // CHUNK, scatter)
 
-    loop(tiles, tile)
+    def group(i):
+        running = [tile(i * PAIR + slot, slot) for slot in range(PAIR)]
+        while running:
+            running = [g for g in running if next(g, True) is None]
+
+    loop(tiles // PAIR, group)
 
     def pack(b):
         swapped = swap_segments([grad_s[v, :, pl.ds(aligned(b, LANES), LANES)] for v in range(VIEWS)])
@@ -520,8 +539,8 @@
     vmem = pl.BlockSpec(memory_space=pltpu.VMEM)
     sems = pltpu.SemaphoreType.DMA((owners,))
     blocks = pltpu.VMEM((owners, FIELDS, LANES), F32)
-    plane = pltpu.VMEM((PIX, length), F32)
-    pair = pltpu.VMEM((2, PIX, length), BF16)
+    plane = pltpu.VMEM((PAIR, PIX, length), F32)
+    pair = pltpu.VMEM((PAIR, 2, PIX, length), BF16)
     image_type = jax.ShapeDtypeStruct((3, tiles, PIX), F32)
     image, returned, raw, wanted = pl.pallas_call(
         splat_kernel,
@@ -549,7 +568,7 @@
             blocks,
             blocks,
             pltpu.VMEM((VIEWS, 3 * ROWS, slots), BF16),
-            pltpu.VMEM((slots, length), BF16),
+            pltpu.VMEM((tiles, slots, length), BF16),
             pltpu.VMEM((VIEWS, ROWS, slots), F32),
             pair, plane, plane, plane, plane, pair, plane, pair,
             pltpu.SemaphoreType.DMA((9,)),

time: 37.4 us -> 34.3 us (0.917)
  Pallas kernels: 36.6 us -> 33.5 us
    pallas_call x1, Pallas kernels: 32.4 us -> 29.4 us  [local(): pl.pallas_call(splat_kernel, in_specs=[pl.BlockSpec(memory_space=pl.ANY)]...]
where the time goes in v3:
time: 34.3 us; the launch traced here: 34.2 us
  Pallas kernels  33.5 us (98%)
  between operations  0.64 us (2%)
    pallas_call x1, Pallas kernels, local(): pl.pallas_call(splat_kernel, in_specs=[pl.BlockSpec(memory_space=pl.ANY)]...  29.4 us
    pallas_call x1, Pallas kernels, local(): pl.pallas_call(pull_kernel, grid=(chunks,), in_specs=[want_spec, block_sp...  4.13 us

profile of v3, /device:TPU:0, one launch (start us, length us, event | category | flops | bytes accessed | tf_op | source)
XLA Modules:
  0.0 34.2 jit_solution(14401934015643732922)
XLA Ops:
  0.6 29.4 %shard_map.128 = (f32[3,8,256]{2,1,0:T(8,128)}, f32[16,9,128]{2,1,0:T(8,128)}, f32[64,512]{1,0:T(8,128)}, s32[1,512]{1,0:T(1,128)}) custom-call(s32[4,1,128]{2,1,0:T(1,128)} %bitcast.4, f32[3,4096]{1,0:T(4,128)} %cen_hbm.1, f32[9,4096]{1,0:T(8,128)} %fac_hbm.1, f32[48,4096]{1,0:T(8,128)} %har_hbm.1, f32[1,4096]{1,0:T(1,128)} %bitcast.3, f32[4,3]{1,0:T(4,128)} %cam_ref.1, ...), custom_call_target="tpu_custom_call" | custom-call | tf_op jit(solution)/shard_map/pallas_call | solution.py:545
  30.1 4.1 %shard_map.129 = (f32[3,4096]{1,0:T(4,128)}, f32[9,4096]{1,0:T(8,128)}, f32[48,4096]{1,0:T(8,128)}, f32[1,4096]{1,0:T(1,128)}, f32[3,8,256]{2,1,0:T(8,128)}) custom-call(s32[1,512]{1,0:T(1,128)} %get-tuple-element.14.want_ref, f32[16,9,128]{2,1,0:T(8,128)} %get-tuple-element.15.back_ref, f32[64,512]{1,0:T(8,128)} %get-tuple-element.16.raw_ref, ...), custom_call_target="tpu_custom_call" | custom-call | tf_op jit(solution)/shard_map/pallas_call | solution.py:584

commit v4 on v3

--- a/solution.py
+++ b/solution.py
@@ -24,7 +24,7 @@
 BF16 = jnp.bfloat16
 VMEM_LIMIT = 60 * 1024 * 1024
 FIELDS = 9
-PAIR = 2
+PAIR = 4
 LOG2E = 1.4426950408889634
 
 BAND_ONE = 0.4886025119029199

time: 34.3 us -> 33.9 us (0.988)
  Pallas kernels: 33.5 us -> 33.1 us
    pallas_call x1, Pallas kernels: 29.4 us -> 28.9 us  [local(): pl.pallas_call(splat_kernel, in_specs=[pl.BlockSpec(memory_space=pl.ANY)]...]
where the time goes in v4:
time: 33.9 us; the launch traced here: 33.7 us
  Pallas kernels  33.1 us (98%)
  between operations  0.64 us (2%)
    pallas_call x1, Pallas kernels, local(): pl.pallas_call(splat_kernel, in_specs=[pl.BlockSpec(memory_space=pl.ANY)]...  28.9 us
    pallas_call x1, Pallas kernels, local(): pl.pallas_call(pull_kernel, grid=(chunks,), in_specs=[want_spec, block_sp...  4.13 us

profile of v4, /device:TPU:0, one launch (start us, length us, event | category | flops | bytes accessed | tf_op | source)
XLA Modules:
  0.0 33.7 jit_solution(17772889025851050260)
XLA Ops:
  0.6 28.9 %shard_map.128 = (f32[3,8,256]{2,1,0:T(8,128)}, f32[16,9,128]{2,1,0:T(8,128)}, f32[64,512]{1,0:T(8,128)}, s32[1,512]{1,0:T(1,128)}) custom-call(s32[4,1,128]{2,1,0:T(1,128)} %bitcast.4, f32[3,4096]{1,0:T(4,128)} %cen_hbm.1, f32[9,4096]{1,0:T(8,128)} %fac_hbm.1, f32[48,4096]{1,0:T(8,128)} %har_hbm.1, f32[1,4096]{1,0:T(1,128)} %bitcast.3, f32[4,3]{1,0:T(4,128)} %cam_ref.1, ...), custom_call_target="tpu_custom_call" | custom-call | tf_op jit(solution)/shard_map/pallas_call | solution.py:545
  29.6 4.1 %shard_map.129 = (f32[3,4096]{1,0:T(4,128)}, f32[9,4096]{1,0:T(8,128)}, f32[48,4096]{1,0:T(8,128)}, f32[1,4096]{1,0:T(1,128)}, f32[3,8,256]{2,1,0:T(8,128)}) custom-call(s32[1,512]{1,0:T(1,128)} %get-tuple-element.14.want_ref, f32[16,9,128]{2,1,0:T(8,128)} %get-tuple-element.15.back_ref, f32[64,512]{1,0:T(8,128)} %get-tuple-element.16.raw_ref, ...), custom_call_target="tpu_custom_call" | custom-call | tf_op jit(solution)/shard_map/pallas_call | solution.py:584
